TPU v7x, 32 devices: a whole 2x2x4 slice. The times are simulated.
32 devices in a mesh: seq: 8 (over z, y), head: 4 (over x, core).
Axes of the slice: x: 2, y: 2, z: 4, core: 2. Of those that a mesh axis runs over, the one named last changes fastest.
Arguments:
- tokens: bfloat16 [16384, 512], P(('seq', 'head')), may hold values from -6 to 6
- lengths: int32 [3], replicated, may hold values from 512 to 14336, as said below
- feature_seed: int32 [1], replicated, may hold values from 0 to 1048575
- norm_gain: bfloat16 [512], P('seq'), may hold values from 0.5 to 1.5
- norm_shift: bfloat16 [512], P('seq'), may hold values from -1.5 to 1.5
- query_weight: bfloat16 [512, 512], P('seq', 'head'), may hold values from -0.25 to 0.25
- key_weight: bfloat16 [512, 512], P('seq', 'head'), may hold values from -0.25 to 0.25
- value_weight: bfloat16 [512, 512], P('seq', 'head'), may hold values from -0.25 to 0.25
- gate_weight: bfloat16 [512, 8], P('seq', 'head'), may hold values from -0.25 to 0.25
- gate_bias: float32 [8], P('head'), may hold values from 3.5 to 14
- out_weight: bfloat16 [512, 512], P('head', 'seq'), may hold values from -0.75 to 0.75
- ffn_gain: bfloat16 [512], P('seq'), may hold values from 0.5 to 1.5
- ffn_shift: bfloat16 [512], P('seq'), may hold values from -1.5 to 1.5
- up_weight: bfloat16 [512, 2048], P('seq', 'head'), may hold values from -0.25 to 0.25
- down_weight: bfloat16 [2048, 512], P('head', 'seq'), may hold values from -0.125 to 0.125
- cotangent: bfloat16 [16384, 512], P(('seq', 'head')), may hold values from -6 to 6
Outputs:
- result: bfloat16 [16384, 512], P(('seq', 'head'))
- grad_tokens: float32 [16384, 512], P(('seq', 'head'))
- grad_norm_gain: float32 [512], P('seq')
- grad_norm_shift: float32 [512], P('seq')
- grad_query_weight: float32 [512, 512], P('seq', 'head')
- grad_key_weight: float32 [512, 512], P('seq', 'head')
- grad_value_weight: float32 [512, 512], P('seq', 'head')
- grad_gate_weight: float32 [512, 8], P('seq', 'head')
- grad_gate_bias: float32 [8], P('head')
- grad_out_weight: float32 [512, 512], P('head', 'seq')
- grad_ffn_gain: float32 [512], P('seq')
- grad_ffn_shift: float32 [512], P('seq')
- grad_up_weight: float32 [512, 2048], P('seq', 'head')
- grad_down_weight: float32 [2048, 512], P('head', 'seq')
Inputs may be any that keep to these rules, and one draw needn't show every extreme that they name: `lengths`: the documents lie end to end from the first token; the tokens from filled on are padding, at least two. Two entries are sentences of 512 to 1023 tokens; the other, second or third in the list, is one document of exactly 14336 tokens, which begins among the first 2048 tokens and ends among the last 2048.
All inputs are finite; a program needn't handle non-finite values.
Results may differ from a plain program's by a relative error of at most 0.02.
The roundings to bfloat16 on the way count: a program that leaves them out, or rounds other values in their place, can miss the bound.
Values may be sent and summed in bfloat16 or wider, within the bound.
A program may use at most 128 MiB of HBM per device.

v0:
```python
import functools
import math

import jax
import jax.numpy as jnp
from jax import lax
from jax.experimental import pallas as pl
from jax.experimental.pallas import tpu as pltpu
from jax.sharding import PartitionSpec as P

BF, F32, I32 = jnp.bfloat16, jnp.float32, jnp.int32
MESH = pl.DeviceIdType.MESH
HEADS, HEAD_DIM, FEATS = 8, 64, 128
PAIRS = HEADS // 2
LANES = 128
EPS, FLOOR2, GATE_PEN = 1e-5, 0.0625, 0.5
TABLE_SCALE = 1.0 / math.sqrt(21845.0)
FEAT_SCALE = 1.0 / math.sqrt(FEATS)
INV_TWO_PI, TWO_PI = 1.0 / (2.0 * math.pi), 2.0 * math.pi
SIN = (0.9999996027571254, -0.16666553170295112, 0.008332405799301931, -0.00019808693226998236,
       2.6997700314773084e-06, -2.036409109746239e-08)
COS = (0.9999992193982472, -0.4999942543676011, 0.04165980908449851, -0.0013858873219640337,
       2.420384320646774e-05, -2.1976364824224383e-07)
ERFC = (0.254829592, -0.284496736, 1.421413741, -1.453152027, 1.061405429)
ATT = 4 * LANES
KEY, SMALL, VALUE, QUERY = (slice(i * LANES, (i + 1) * LANES) for i in range(4))
NORMAL, DECAY, STATE_ROWS = HEAD_DIM, HEAD_DIM + 1, HEAD_DIM + 8
STATES = (HEADS, STATE_ROWS, 2 * FEATS)
VMEM_BYTES = 56 * 1024 * 1024
LAYER_BYTES = 63 * 1024 * 1024


def nn(a, b):
    return lax.dot_general(a, b, (((1,), (0,)), ((), ())), preferred_element_type=F32)


def nt(a, b):
    return lax.dot_general(a, b, (((1,), (1,)), ((), ())), preferred_element_type=F32)


def tn(a, b):
    return lax.dot_general(a, b, (((0,), (0,)), ((), ())), preferred_element_type=F32)


def halves(x, axis=1):
    hi = x.astype(BF)
    return jnp.concatenate([hi, (x - hi.astype(F32)).astype(BF)], axis=axis)


def iota(shape, dim):
    return lax.broadcasted_iota(I32, shape, dim)


def rows_loop(total, step, body):
    body(pl.ds(0, total), 0, total)


def pair_loop(body):
    def one(p, carry):
        body(p)
        return carry

    lax.fori_loop(0, PAIRS, one, 0)


def head_ones(rows, cols, row_span, col_span):
    same = (iota((rows, cols), 0) // row_span) % 2 == iota((rows, cols), 1) // col_span
    return jnp.where(same, 1.0, 0.0).astype(BF)


def marks(pos, base, lengths_ref):
    start = jnp.int32(0)
    segment = jnp.zeros(pos.shape, I32)
    reset = jnp.zeros(pos.shape, F32)
    carry = jnp.ones(pos.shape, F32)
    for d in range(lengths_ref.shape[0]):
        segment = segment + jnp.where(pos >= start, 1, 0)
        reset = jnp.where(pos == start, 1.0, reset)
        carry = jnp.where((pos >= start) & (pos - start <= pos - base), 0.0, carry)
        start = start + lengths_ref[d]
    live = jnp.where(pos < start, 1.0, 0.0)
    segment = segment + jnp.where(pos >= start, 1, 0)
    return segment, reset, live, carry, start


def horner(coefs, t):
    acc = jnp.full_like(t, coefs[-1])
    for c in coefs[-2::-1]:
        acc = acc * t + c
    return acc


def sincos(angle):
    r = angle - jnp.round(angle * INV_TWO_PI) * TWO_PI
    t = r * r
    return r * horner([c * FEAT_SCALE for c in SIN], t), horner([c * FEAT_SCALE for c in COS], t)


def gelu_parts(x):
    t = 1.0 / (1.0 + (0.3275911 / math.sqrt(2.0)) * jnp.abs(x))
    e = jnp.exp(-0.5 * x * x)
    q = 0.5 * t * horner(ERFC, t) * e
    cdf = jnp.where(x < 0.0, q, 1.0 - q)
    return x * cdf, cdf + x * e * (1.0 / math.sqrt(2.0 * math.pi))


def norm_stats(x):
    center = jnp.mean(x, axis=-1, keepdims=True)
    spread = jnp.mean(x * x, axis=-1, keepdims=True) - center * center
    inv = lax.rsqrt(spread + EPS)
    return (x - center) * inv, inv


def norm_back(grad, xhat, inv, gain):
    p = grad * gain
    return inv * (p - jnp.mean(p, axis=-1, keepdims=True) - xhat * jnp.mean(p * xhat, axis=-1, keepdims=True))


def by_eight(x):
    return jnp.sum(x.reshape(x.shape[0] // 8, 8, x.shape[1]), axis=0)


def panel(ref, p, cols):
    x = ref[p, :, :, :, cols]
    return x.reshape(x.shape[0] * x.shape[1] * x.shape[2], x.shape[3])


def low_lanes(rows):
    return iota((rows, LANES), 1) < HEAD_DIM


def widen(pair, a):
    return pair[:, a * HEAD_DIM : a * HEAD_DIM + 1]


def head_values(v, a, low):
    one = jnp.ones_like(v)
    return jnp.where(low, v, one) if a == 0 else jnp.where(low, one, v)


def state_of(states, p, a):
    own = states[2 * p + a, 0:HEAD_DIM, :]
    rest = jnp.broadcast_to(states[2 * p + a, NORMAL : NORMAL + 1, :], own.shape)
    return jnp.concatenate([own, rest] if a == 0 else [rest, own], axis=0)


def put_state(states, h, own, normal, decay):
    states[h, 0:HEAD_DIM, :] = own
    rest = jnp.zeros((STATE_ROWS - DECAY - 1, 2 * FEATS), F32)
    states[h, NORMAL:, :] = jnp.concatenate([normal, twice(decay), rest], axis=0)


def twice(x):
    return jnp.concatenate([x, x], axis=1)


def run_pairs(body, hook, order=None):
    def one(p):
        body(order(p) if order else p)
        for at, acts in (hook or {}).items():

            @pl.when(p == at)
            def _():
                for act, *given in acts:
                    act(*given)

    pair_loop(one)


def tables(T, base, r):
    pos = base + iota((8, T), 1)
    seg_row, _, live_row, _, _ = marks(pos, base, r.lengths)
    seg1, live1, pos1 = seg_row[0:1], live_row[0:1], pos[0:1]

    def mask_rows(rows, at, n):
        row_pos = base + at + iota((n, 1), 0)
        seg_col = marks(row_pos, base, r.lengths)[0]
        allowed = (seg_col == seg1) & (pos1 <= row_pos) & (live1 > 0.0)
        r.mask[rows, :] = jnp.where(allowed, 0.0, -1e30)

    rows_loop(T, 64, mask_rows)
    hash_seed = r.seed[0] * jnp.int32(-2048144789)

    def table(p):
        place = (p * LANES + iota((LANES, LANES), 0)) * FEATS + iota((LANES, LANES), 1)
        y = place * jnp.int32(-1640531535) + hash_seed
        y = y ^ lax.shift_right_logical(y, jnp.int32(15))
        y = y * jnp.int32(739982445)
        y = y ^ lax.shift_right_logical(y, jnp.int32(13))
        y = y * jnp.int32(695872825)
        y = y ^ lax.shift_right_logical(y, jnp.int32(16))
        s = jnp.full(y.shape, -510, I32)
        for k in range(4):
            s = s + (lax.shift_right_logical(y, jnp.int32(8 * k)) & jnp.int32(255))
        top = iota((LANES, LANES), 0) < HEAD_DIM
        odd = s & 1

        def diagonal(x):
            x = x.astype(F32)
            return jnp.concatenate([jnp.where(top, x, 0.0), jnp.where(top, 0.0, x)], axis=1).astype(BF)

        r.tab[p, 0:LANES, :] = diagonal(s - odd)
        r.tab[p, LANES:, :] = diagonal(odd)
        r.tabn[p] = diagonal(s)

    pair_loop(table)


def first_norm(T, base, r):
    pick = jnp.where(iota((16, LANES), 0) == iota((16, LANES), 1), 1.0, 0.0).astype(BF)
    for p in range(PAIRS):
        rows = nt(pick, panel(r.ga, p, SMALL))
        r.gate[2 * p : 2 * p + 2, :] = rows[0:2]
        r.gate[8 + 2 * p : 10 + 2 * p, :] = rows[0:2]
        r.bias[2 * p : 2 * p + 1, :] = rows[6:7] + rows[7:8] + rows[8:9]
        r.bias[2 * p + 1 : 2 * p + 2, :] = rows[9:10] + rows[10:11] + rows[11:12]
        if p == 0:
            r.vec[...] = rows[0:8]

    def norm_rows(rows, at, n):
        xhat, _ = norm_stats(r.tok[rows, :].astype(F32))
        r.normed[rows, :] = (xhat * r.vec[2:3, :] + r.vec[3:4, :]).astype(BF)

    rows_loop(T, 64, norm_rows)
    logits = nt(r.gate[...].astype(BF), r.normed[...])[0:8] + r.bias[:, 0:1]
    r.logits[...] = logits
    pos = base + iota((8, T), 1)
    _, reset_row, live_row, carry_row, _ = marks(pos, base, r.lengths)
    decay = -(jnp.log1p(jnp.exp(-jnp.abs(logits))) + jnp.maximum(-logits, 0.0)) * live_row * (1.0 - reset_row)
    run = decay
    lane = iota((8, T), 1)
    shift = 1
    while shift < T:
        run = run + jnp.where(lane >= shift, pltpu.roll(run, shift, 1), 0.0)
        shift *= 2
    r.run[...] = run
    r.total[...] = jnp.broadcast_to(jnp.exp(run[:, T - 1 : T]) * carry_row[:, T - 1 : T], (8, LANES))
    hi = run.astype(BF).astype(F32)
    mid = (run - hi).astype(BF).astype(F32)
    run3 = jnp.concatenate([hi, mid, run - hi - mid, jnp.zeros_like(hi)], axis=0).astype(BF)

    def spread(p):
        chosen = iota((32, LANES), 0) % 8 == 2 * p + iota((32, LANES), 1) // HEAD_DIM
        r.rb[p] = tn(run3, jnp.where(chosen, 1.0, 0.0).astype(BF))

    pair_loop(spread)


def features(T, r, p, u, out):
    ones2 = head_ones(2 * LANES, 2 * LANES, HEAD_DIM, LANES)
    r.s1[...] = nn(jnp.concatenate([u, u], axis=1), r.tab[p])
    uf = u.astype(F32)
    r.s2[...] = nn(halves(uf * uf), ones2)

    def body(rows, at, n):
        s, c = sincos(r.s1[rows, :] * (lax.rsqrt(r.s2[rows, :] + 1e-6) * TABLE_SCALE))
        for a in range(2):
            out[2 * p + a, rows, 0:FEATS] = s[:, a * FEATS : (a + 1) * FEATS].astype(BF)
            out[2 * p + a, rows, FEATS : 2 * FEATS] = c[:, a * FEATS : (a + 1) * FEATS].astype(BF)

    rows_loop(T, 64, body)


def end_factor(T, base, r):
    last_seg = marks(base + T - 1 + iota((8, LANES), 1) * 0, base, r.lengths)[0][0:1, 0:1]
    seg_col, _, live_col, _, _ = marks(base + iota((T, LANES), 0), base, r.lengths)
    return jnp.where(seg_col == last_seg, live_col, 0.0)


def keys(T, base, r, hook=None):
    def pair(p):
        r.k[p] = nn(r.normed[...], panel(r.ga, p, KEY)).astype(BF)
        features(T, r, p, r.k[p], r.kf)

    run_pairs(pair, hook)


def states(T, base, r):
    end_live = end_factor(T, base, r)

    def pair(p):
        r.v[p] = nn(r.normed[...], panel(r.ga, p, VALUE)).astype(BF)
        decay_end = jnp.exp(r.rb[p, T - 1 : T, :] - r.rb[p]) * end_live
        lane = iota((T, LANES), 1)
        factor = jnp.where(lane < 2, widen(decay_end, 0), widen(decay_end, 1))
        rough = factor.astype(BF).astype(F32)
        factor = jnp.where(lane % 2 == 0, rough, factor - rough)
        ends = tn(factor.astype(BF), jnp.concatenate([r.kf[2 * p], r.kf[2 * p + 1]], axis=1))
        for a in range(2):
            h = 2 * p + a
            scaled = (r.kf[h].astype(F32) * widen(decay_end, a)).astype(BF)
            state = tn(r.v[p], scaled)[a * HEAD_DIM : (a + 1) * HEAD_DIM]
            normal = ends[2 * a : 2 * a + 1, a * 2 * FEATS : (a + 1) * 2 * FEATS]
            normal = normal + ends[2 * a + 1 : 2 * a + 2, a * 2 * FEATS : (a + 1) * 2 * FEATS]
            put_state(r.out, h, state, normal, r.total[pl.ds(h, 1), :])

    pair_loop(pair)


def queries(T, base, r, hook=None):
    low = low_lanes(T)

    def pair(p):
        r.q[p] = nn(r.normed[...], panel(r.ga, p, QUERY)).astype(BF)
        features(T, r, p, r.q[p], r.qf)
        v = r.v[p]
        for a in range(2):
            h = 2 * p + a
            r.s[...] = nt(r.qf[h], r.kf[h])
            run_row = r.run[pl.ds(h, 1), :]

            def body(rows, at, n):
                gap = jnp.minimum(widen(r.rb[p, rows, :], a) - run_row, r.mask[rows, :])
                w = r.s[rows, :] * jnp.exp(gap)
                rounded = w.astype(BF)
                r.w[h, rows, :] = rounded
                rest = jnp.sum(w - rounded.astype(F32), axis=1, keepdims=True)
                r.zfix[p, rows, a * HEAD_DIM : (a + 1) * HEAD_DIM] = jnp.broadcast_to(rest, (n, HEAD_DIM)).astype(BF)

            rows_loop(T, 64, body)
            r.own[h] = nn(r.w[h], head_values(v, a, low))

    run_pairs(pair, hook)


def carry_factor(T, base, r):
    _, _, live_col, carry_col, _ = marks(base + iota((T, LANES), 0), base, r.lengths)
    return live_col, carry_col


def attend(T, base, r):
    low = low_lanes(T)
    live_col, carry_col = carry_factor(T, base, r)

    def join(p):
        factor = jnp.exp(r.rb[p]) * carry_col
        total = []
        for a in range(2):
            h = 2 * p + a
            carried = nt(twice(r.qf[h]), halves(state_of(r.inn, p, a)))
            joined = r.own[h] + widen(factor, a) * carried
            r.joined[h] = joined
            total.append(joined)
        num = jnp.where(low, total[0], total[1])
        z = pltpu.roll(jnp.where(low, total[1], total[0]), HEAD_DIM, 1) + r.zfix[p].astype(F32)
        r.att[p] = (live_col * num * lax.rsqrt(z * z + FLOOR2)).astype(BF)

    pair_loop(join)
    o = out_columns(r)
    branch = None
    for p in range(0, PAIRS, 2):
        part = nt(
            jnp.concatenate([r.att[p], r.att[p + 1]], axis=1),
            jnp.concatenate([panel(r.gf, p, o), panel(r.gf, p + 1, o)], axis=1),
        )
        branch = part if branch is None else branch + part
    r.mid[...] = branch

    def norm_rows(rows, at, n):
        mid = r.mid[rows, :] + r.tok[rows, :].astype(F32)
        r.mid[rows, :] = mid
        xhat, inv = norm_stats(mid)
        r.xhat[rows, :] = xhat
        r.inv[rows, :] = jnp.broadcast_to(inv, (n, LANES))
        r.two[rows, :] = (xhat * r.vec[4:5, :] + r.vec[5:6, :]).astype(BF)

    rows_loop(T, 64, norm_rows)


def feed_columns(r):
    ff = (r.gf.shape[-1] - LANES) // 2
    return slice(LANES + ff, LANES + 2 * ff), slice(LANES, LANES + ff)


def out_columns(r):
    return slice(0, LANES)


def cotangents(T, base, r):
    _, d = feed_columns(r)

    def part(p):
        r.h2[p] = nn(r.cot[...], panel(r.gf, p, d))

    pair_loop(part)


def feed(T, base, r):
    low = low_lanes(T)
    live_col, carry_col = carry_factor(T, base, r)
    r.acc1[...] = jnp.zeros_like(r.acc1)
    r.acc2[...] = jnp.zeros_like(r.acc2)
    u, d = feed_columns(r)
    o = out_columns(r)

    def part(p):
        up, down = panel(r.gf, p, u), panel(r.gf, p, d)
        r.h1[...] = nn(r.two[...], up)

        def body(rows, at, n):
            value, slope = gelu_parts(r.h1[rows, :])
            r.act[p, rows, :] = value.astype(BF)
            r.gh[p, rows, :] = (r.h2[p, rows, :] * slope).astype(BF)

        rows_loop(T, 64, body)
        r.acc1[...] += nt(r.act[p], down)
        r.acc2[...] += nt(r.gh[p], up)

    pair_loop(part)
    r.sums[...] = jnp.zeros_like(r.sums)

    def finish(rows, at, n):
        r.result[rows, :] = (r.mid[rows, :] + r.acc1[rows, :]).astype(BF)
        xhat, gn = r.xhat[rows, :], r.acc2[rows, :]
        r.sums[0:8, :] += by_eight(gn * xhat)
        r.sums[8:16, :] += by_eight(gn)
        back = norm_back(gn, xhat, r.inv[rows, 0:1], r.vec[4:5, :])
        grad = r.cot[rows, :].astype(F32) + back
        r.gmid[rows, :] = grad
        r.gb[rows, :] = grad.astype(BF)

    rows_loop(T, 64, finish)
    r.fsum[0:1, :] = jnp.sum(r.sums[0:8, :], axis=0, keepdims=True)
    r.fsum[1:2, :] = jnp.sum(r.sums[8:16, :], axis=0, keepdims=True)
    ones1 = head_ones(2 * LANES, LANES, HEAD_DIM, HEAD_DIM)
    row_ones = jnp.ones((16, 2 * LANES), BF)
    first_half = iota((T, LANES), 1) % HEAD_DIM < HEAD_DIM // 2

    def back(p):
        g = nn(r.gb[...], panel(r.gf, p, o)).astype(BF).astype(F32) * live_col
        total = [r.joined[2 * p], r.joined[2 * p + 1]]
        num = jnp.where(low, total[0], total[1])
        z = pltpu.roll(jnp.where(low, total[1], total[0]), HEAD_DIM, 1) + r.zfix[p].astype(F32)
        rden = lax.rsqrt(z * z + FLOOR2)
        dn = (g * rden).astype(BF).astype(F32)
        dz = nn(halves(dn * num), ones1) * (z * rden * rden)
        dz = pltpu.roll(dz * (-2.0 / HEAD_DIM), HEAD_DIM, 1)
        rough = dz.astype(BF).astype(F32)
        dz = jnp.where(first_half, rough, dz - rough)
        factor = jnp.exp(r.rb[p]) * carry_col
        for a in range(2):
            h = 2 * p + a
            joint = (jnp.where(low, dn, dz) if a == 0 else jnp.where(low, dz, dn)).astype(BF)
            r.dn[h] = joint
            r.dr[pl.ds(h, 1), :] = nt(row_ones, halves(joint.astype(F32) * total[a]))[0:1]
            adj = tn(joint, (r.qf[h].astype(F32) * widen(factor, a)).astype(BF))
            at, half = (1 - a) * HEAD_DIM, HEAD_DIM // 2
            normal = 0.5 * (adj[at : at + 1] + adj[at + half : at + half + 1])
            put_state(r.adj, h, adj[a * HEAD_DIM : (a + 1) * HEAD_DIM], normal, r.total[pl.ds(h, 1), :])

    pair_loop(back)


def up_grads(T, base, r):
    up, _ = feed_columns(r)
    pair_loop(lambda p: put_panel(r.ggf, p, up, tn(r.two[...], r.gh[p])))


def down_grads(T, base, r):
    _, down = feed_columns(r)

    def part(p):
        put_panel(r.ggf, p, down, tn(r.cot[...], r.act[p]))
        put_panel(r.ggf, p, out_columns(r), tn(r.gb[...], r.att[p]))

    pair_loop(part)


def put_panel(ref, p, cols, x):
    shape = ref.shape[1:4] + (x.shape[1],)
    ref[p, :, :, :, cols] = x.astype(BF).reshape(shape)


def back(T, base, r, tokens_all, near_hook=None, between=lambda: None, far_hook=None, order=None):
    D = r.tok.shape[1]
    low = low_lanes(T)
    _, carry_col = carry_factor(T, base, r)
    end_live = end_factor(T, base, r)
    ones1 = head_ones(2 * LANES, LANES, HEAD_DIM, HEAD_DIM)
    row_ones = jnp.ones((16, 2 * LANES), BF)
    r.acc1[...] = jnp.zeros_like(r.acc1)

    def feature_back(p, u, da):
        ds = nt(da, r.tabn[p]) * TABLE_SCALE
        uf = u.astype(F32)
        inv = lax.rsqrt(nn(halves(uf * uf), ones1) + 1e-6)
        uh = uf * inv
        return (inv * (ds - uh * nn(halves(uh * ds), ones1))).astype(BF)

    def angles(rows, source, feat, h):
        x, f = source[rows, :], feat[h, rows, :].astype(F32)
        return x[:, :FEATS] * f[:, FEATS:] - x[:, FEATS:] * f[:, :FEATS]

    def near(p):
        v = r.v[p]
        factor = jnp.exp(r.rb[p]) * carry_col
        for a in range(2):
            h = 2 * p + a
            r.s[...] = nt(r.dn[h], head_values(v, a, low))
            run_row = r.run[pl.ds(h, 1), :]

            def body(rows, at, n):
                gap = jnp.minimum(widen(r.rb[p, rows, :], a) - run_row, r.mask[rows, :])
                r.ds[rows, :] = (r.s[rows, :] * jnp.exp(gap)).astype(BF)

            rows_loop(T, 64, body)
            before = halves(state_of(r.inn, p, a), 0)
            r.s1[...] = nn(r.ds[...], r.kf[h]) + widen(factor, a) * nn(twice(r.dn[h]), before)
            r.s2[...] = tn(r.ds[...], r.qf[h])
            r.ghv[h] = tn(r.w[h], r.dn[h])

            def turn(rows, at, n):
                r.da[p, rows, a * FEATS : (a + 1) * FEATS] = angles(rows, r.s1, r.qf, h).astype(BF)
                r.da[p, rows, (2 + a) * FEATS : (3 + a) * FEATS] = angles(rows, r.s2, r.kf, h).astype(BF)

            rows_loop(T, 64, turn)
        grad = feature_back(p, r.q[p], r.da[p, :, : 2 * FEATS])
        r.acc1[...] += nt(grad, panel(r.ga, p, QUERY))
        put_panel(r.gga, p, slice(2 * LANES, 3 * LANES), tn(r.normed[...], grad))

    def far(p):
        v = r.v[p]
        decay_end = jnp.exp(r.rb[p, T - 1 : T, :] - r.rb[p]) * end_live
        grad_v = []
        for a in range(2):
            h = 2 * p + a
            end, hv = state_of(r.aend, p, a), head_values(v, a, low)
            late = widen(decay_end, a) * nt(twice(r.kf[h]), halves(end))
            r.s2[...] = widen(decay_end, a) * nn(twice(hv), halves(end, 0))
            grad_hv = r.ghv[h] + late
            grad_v.append(grad_hv)

            def turn(rows, at, n):
                lanes = slice((2 + a) * FEATS, (3 + a) * FEATS)
                r.da[p, rows, lanes] = (r.da[p, rows, lanes].astype(F32) + angles(rows, r.s2, r.kf, h)).astype(BF)

            rows_loop(T, 64, turn)
            hvf = hv.astype(F32)
            k_side = nt(row_ones, halves(hvf * grad_hv))
            r.drun[pl.ds(h, 1), :] = r.dr[pl.ds(h, 1), :] - k_side[0:1]
            owed = jnp.sum(end * state_of(r.inn, p, a), axis=0, keepdims=True)
            owed = r.total[pl.ds(h, 1), 0:1] * jnp.sum(owed, axis=1, keepdims=True)
            owed = owed + jnp.sum(jnp.sum(hvf * late, axis=0, keepdims=True), axis=1, keepdims=True)
            r.owed[pl.ds(h, 1), :] = jnp.broadcast_to(owed, (1, LANES))
        grad_v = jnp.where(low, grad_v[0], grad_v[1]).astype(BF)
        grads = jnp.concatenate([feature_back(p, r.k[p], r.da[p, :, 2 * FEATS :]), grad_v], axis=1)
        weights = jnp.concatenate([panel(r.ga, p, KEY), panel(r.ga, p, VALUE)], axis=1)
        r.acc1[...] += nt(grads, weights)
        put_panel(r.gga, p, slice(0, 2 * LANES), tn(r.normed[...], grads))

    run_pairs(near, near_hook, order)
    between()
    run_pairs(far, far_hook, order)
    pos = base + iota((8, T), 1)
    _, reset_row, live_row, _, filled = marks(pos, base, r.lengths)
    lane = iota((8, T), 1)
    run = r.drun[...]
    shift = 1
    while shift < T:
        run = run + jnp.where(lane < T - shift, pltpu.roll(run, T - shift, 1), 0.0)
        shift *= 2
    grad_decay = run + r.owed[:, 0:1]
    logits = r.logits[...]
    e = jnp.exp(-jnp.abs(logits))
    small, large = e / (1.0 + e), 1.0 / (1.0 + e)
    gate = jnp.where(logits >= 0.0, large, small)
    rest = jnp.where(logits >= 0.0, small, large)
    penalty = GATE_PEN * tokens_all / HEADS / jnp.broadcast_to(filled, (8, T)).astype(F32)
    grad_logits = grad_decay * live_row * (1.0 - reset_row) * rest + penalty * live_row * gate * rest
    both = halves(grad_logits, 0)
    r.acc1[...] += tn(both, r.gate[...].astype(BF))
    gate_rows = nn(both, r.normed[...])
    gate_rows = gate_rows[0:8] + gate_rows[8:16]
    bias = jnp.broadcast_to(jnp.sum(grad_logits, axis=1, keepdims=True), (8, D))
    r.sums[...] = jnp.zeros_like(r.sums)

    def finish(rows, at, n):
        xhat, inv = norm_stats(r.tok[rows, :].astype(F32))
        gn = r.acc1[rows, :]
        r.sums[0:8, :] += by_eight(gn * xhat)
        r.sums[8:16, :] += by_eight(gn)
        r.gtok[rows, :] = r.gmid[rows, :] + norm_back(gn, xhat, inv, r.vec[2:3, :])

    rows_loop(T, 64, finish)
    norm_gain = jnp.sum(r.sums[0:8, :], axis=0, keepdims=True)
    norm_shift = jnp.sum(r.sums[8:16, :], axis=0, keepdims=True)
    lines = [norm_gain, norm_shift, r.fsum[0:2, :]]
    for p in range(PAIRS):
        rows = jnp.concatenate([gate_rows[2 * p : 2 * p + 2]] + lines + [bias[2 * p : 2 * p + 2]], axis=0)
        for g in range(D // LANES):
            r.lines[p, g] = rows[:, g * LANES : (g + 1) * LANES]


class Refs:
    def __init__(self, **refs):
        self.__dict__.update(refs)


def buffers(T, D, att, rest, ff, seq):
    z = (PAIRS, seq // 2, 2, D // seq)
    pair = (PAIRS, T, LANES)
    return {
        "ga": (z + (att,), BF), "gf": (z + (rest,), BF), "gga": (z + (att - LANES,), BF), "ggf": (z + (rest,), BF),
        "gate": ((16, D), F32), "bias": ((8, D), F32), "vec": ((8, D), F32), "normed": ((T, D), BF),
        "logits": ((8, T), F32), "run": ((8, T), F32), "total": ((8, LANES), F32), "mask": ((T, T), F32),
        "s1": ((T, 2 * FEATS), F32), "s2": ((T, 2 * FEATS), F32), "s": ((T, T), F32),
        "tab": ((PAIRS, 2 * LANES, 2 * FEATS), BF), "tabn": ((PAIRS, LANES, 2 * FEATS), BF),
        "q": (pair, BF), "k": (pair, BF), "v": (pair, BF), "rb": (pair, F32),
        "qf": ((HEADS, T, 2 * FEATS), BF), "kf": ((HEADS, T, 2 * FEATS), BF),
        "out": (STATES, F32), "inn": (STATES, F32), "adj": (STATES, F32), "aend": (STATES, F32),
        "w": ((HEADS, T, T), BF), "own": ((HEADS, T, LANES), F32), "joined": ((HEADS, T, LANES), F32),
        "att": (pair, BF), "zfix": (pair, BF), "mid": ((T, D), F32), "xhat": ((T, D), F32), "inv": ((T, LANES), F32), "two": ((T, D), BF),
        "acc1": ((T, D), F32), "acc2": ((T, D), F32), "h1": ((T, ff), F32), "h2": ((PAIRS, T, ff), F32),
        "act": ((PAIRS, T, ff), BF), "gh": ((PAIRS, T, ff), BF), "sums": ((16, D), F32), "fsum": ((8, D), F32),
        "result": ((T, D), BF), "gmid": ((T, D), F32), "gb": ((T, D), BF), "dr": ((8, T), F32),
        "dn": ((HEADS, T, LANES), BF), "ds": ((T, T), BF), "da": ((PAIRS, T, 4 * FEATS), BF), "ghv": ((HEADS, T, LANES), F32),
        "lines": ((PAIRS, D // LANES, 8, LANES), F32),
        "drun": ((8, T), F32), "owed": ((8, LANES), F32), "gtok": ((T, D), F32),
    }


FRONT = (
    ("ga",),
    ("gate", "vec", "normed", "logits", "run", "total", "mask", "tabn", "q", "k", "v", "rb", "qf", "kf", "out", "w", "own", "zfix"),
    ("bias", "s1", "s2", "s", "tab"),
)
MIDDLE = (
    ("gf", "vec", "rb", "qf", "own", "zfix", "inn", "total"),
    ("ggf", "result", "gmid", "fsum", "dr", "dn", "adj"),
    ("joined", "att", "mid", "xhat", "inv", "two", "acc1", "acc2", "h1", "h2", "act", "gh", "sums", "gb"),
)
BACK = (
    ("ga", "gate", "vec", "normed", "logits", "run", "total", "mask", "tabn", "q", "k", "v", "rb", "qf", "kf",
     "w", "inn", "aend", "gmid", "fsum", "dr", "dn"),
    ("gga", "gtok", "lines"),
    ("s", "s1", "s2", "ds", "da", "ghv", "drun", "owed", "acc1", "sums"),
)
SHARED = {"joined": "own", "h1": "s", "gmid": "mid", "ds": "gb", "adj": "out", "da": "act", "ghv": "own"}


def front(T, base, r):
    tables(T, base, r)
    first_norm(T, base, r)
    keys(T, base, r)
    states(T, base, r)
    queries(T, base, r)


def middle(T, base, r):
    cotangents(T, base, r)
    attend(T, base, r)
    feed(T, base, r)
    up_grads(T, base, r)
    down_grads(T, base, r)


def here(T):
    return (lax.axis_index("seq") * lax.axis_size("head") + lax.axis_index("head")) * T


def stage(which, names, specs, outer, args, state):
    reads, writes, scratch = names
    shape = lambda n: jax.ShapeDtypeStruct(*specs[n])
    vmem, smem = pl.BlockSpec(memory_space=pltpu.VMEM), pl.BlockSpec(memory_space=pltpu.SMEM)

    def kernel(*refs):
        base_ref, lengths, seed, tok, cot = refs[:5]
        rest = dict(zip(reads + writes + scratch, refs[5:]))
        which(base_ref[0], Refs(lengths=lengths, seed=seed, tok=tok, cot=cot, **rest))

    out = pl.pallas_call(
        kernel,
        out_shape=[shape(n) for n in writes],
        in_specs=[smem] * 3 + [vmem] * (2 + len(reads)),
        out_specs=[vmem] * len(writes),
        scratch_shapes=[pltpu.VMEM(*specs[n]) for n in scratch],
        compiler_params=pltpu.CompilerParams(vmem_limit_bytes=VMEM_BYTES),
        name=outer,
    )(*args, *[state[n] for n in reads])
    state.update(zip(writes, out))


def scan_states(out, reverse):
    seq, head = lax.axis_size("seq"), lax.axis_size("head")
    count = seq * head
    me = lax.axis_index("seq") * head + lax.axis_index("head")
    state = (out[:, DECAY : DECAY + 1, 0:1], out[:, :DECAY])
    step = 1
    order = lambda pairs: [(b, a) for a, b in pairs] if reverse else pairs
    axes = ("seq", "head")
    while step < count:
        moved = jax.tree.map(lambda x: lax.ppermute(x, axes, order([(i, i + step) for i in range(count - step)])), state)
        has = (me < count - step) if reverse else (me >= step)
        f, m = state
        state = (jnp.where(has, f * moved[0], f), m + jnp.where(has, f * moved[1], 0.0))
        step *= 2
    moved = lax.ppermute(state[1], axes, order([(i, i + 1) for i in range(count - 1)]))
    return jnp.concatenate([moved, jnp.zeros((HEADS, STATE_ROWS - DECAY, 2 * FEATS), F32)], axis=1)


def remote(src, dst, send, recv, to):
    return pltpu.make_async_remote_copy(
        src_ref=src, dst_ref=dst, send_sem=send, recv_sem=recv, device_id=to, device_id_type=MESH
    )


class Place:
    def __init__(self):
        self.seq, self.head = lax.axis_size("seq"), lax.axis_size("head")
        s, h = lax.axis_index("seq"), lax.axis_index("head")
        self.z, self.y, self.x, self.c = s // 2, s % 2, h // 2, h % 2
        self.depth = self.seq // 2
        self.count = self.seq * self.head
        self.me = s * self.head + h

    def device(self, z=None, y=None, x=None, c=None):
        pick = lambda given, own: own if given is None else given
        z, y, x, c = pick(z, self.z), pick(y, self.y), pick(x, self.x), pick(c, self.c)
        return (z * 2 + y, x * 2 + c)

    def number(self, i):
        return (i // self.head, i % self.head)

    def around(self, k):
        return (self.z + k) % self.depth

class Semaphores:
    def __init__(self, send, recv):
        self.send, self.recv, self.used = send, recv, 0

    def copy(self, src, dst, to):
        i = self.used
        self.used += 1
        return remote(src, dst, self.send.at[i], self.recv.at[i], to)


GATHER_COPIES = 2 * (3 + 1 + 2 + 2)
SCATTER_COPIES = 2 + 2 * (1 + 1 + 3)


def gather_stages(place, g, lanes, sems):
    half = g.shape[3] // 2
    z, y, x, c = place.z, place.y, place.x, place.c
    pair = x * 2 + c
    stages = [[], [], [], []]
    for part in range(2):
        rows = pl.ds(part * half, half)
        same = lambda ref, to: sems.copy(ref, ref, to)
        for k in range(1, place.depth):
            stages[0].append(same(g.at[pair, z, y, rows, lanes], place.device(z=place.around(k))))
        to_y, to_x = place.device(y=1 - y), place.device(x=1 - x)
        if part == 0:
            stages[1].append(same(g.at[pair, :, y, rows, lanes], to_y))
            stages[2].append(same(g.at[pair, :, :, rows, lanes], to_x))
        else:
            stages[1].append(same(g.at[pair, :, y, rows, lanes], to_x))
            for other in range(2):
                stages[2].append(same(g.at[other * 2 + c, :, y, rows, lanes], to_y))
        for other in range(2):
            stages[3].append(same(g.at[other * 2 + c, :, :, rows, lanes], place.device(c=1 - c)))
    return stages


def begin(stage):
    for copy in stage:
        copy.start()


def arrived(stage):
    for copy in stage:
        copy.wait_recv()


def sent(*stages):
    for stage in stages:
        for copy in stage:
            copy.wait_send()


class Gather:
    def __init__(self, place, ga, gf, sems):
        ff = (gf.shape[-1] - LANES) // 2
        lanes = lambda first, count: pl.ds(first, count)
        self.chunks = [
            gather_stages(place, ref, part, sems)
            for ref, part in (
                (ga, lanes(0, 2 * LANES)),
                (ga, lanes(2 * LANES, 2 * LANES)),
                (gf, lanes(0, LANES + ff)),
                (gf, lanes(LANES + ff, ff)),
            )
        ]

    def begin(self, chunk):
        begin(self.chunks[chunk][0])

    def step(self, chunk, stage):
        arrived(self.chunks[chunk][stage])
        if stage < 3:
            begin(self.chunks[chunk][stage + 1])

    def finish(self):
        for chunk in self.chunks:
            sent(*chunk)


def add_blocks(to, others, count, where):
    def one(i, carry):
        at = where(i)
        total = to[at].astype(F32)
        for ref, index in others:
            total = total + ref[index(i)].astype(F32)
        to[at] = total.astype(to.dtype)
        return carry

    lax.fori_loop(0, count, one, 0)


class Scatter:
    def __init__(self, place, gg, lanes, out, buf, sems):
        self.place, self.gg, self.lanes, self.out = place, gg, lanes, out
        self.r1, self.r2a, self.r2b, self.r3a, self.r3b, self.r4a, self.r4b = buf
        z, y, x, c, n = place.z, place.y, place.x, place.c, place.depth
        self.half = half = gg.shape[3] // 2
        first, last = pl.ds(0, half), pl.ds(half, half)
        other, to_y, to_x = place.device(c=1 - c), place.device(y=1 - y), place.device(x=1 - x)
        self.stages = [
            [sems.copy(gg.at[i * 2 + 1 - c, :, :, :, lanes], self.r1.at[i], other) for i in range(2)],
            [
                sems.copy(self.r1.at[1 - x, :, :, first], self.r2a, to_x),
                sems.copy(self.r1.at[:, :, 1 - y, last], self.r2b, to_y),
            ],
            [sems.copy(self.r2a.at[:, 1 - y], self.r3a, to_y), sems.copy(self.r2b.at[1 - x], self.r3b, to_x)],
            [
                sems.copy(ref.at[place.around(k)], slots.at[k - 1], place.device(z=place.around(k)))
                for ref, slots in ((self.r3a, self.r4a), (self.r3b, self.r4b))
                for k in range(1, n)
            ],
        ]

    def start(self):
        begin(self.stages[0])

    def step(self, i):
        place, n, half = self.place, self.place.depth, self.half
        y, x, c = place.y, place.x, place.c
        first, last = slice(0, half), slice(half, 2 * half)
        lanes = self.lanes
        arrived(self.stages[i])
        if i == 0:
            block = lambda j: (j // (2 * n), (j // 2) % n, j % 2)
            add_blocks(self.r1, [(self.gg, lambda j: ((j // (2 * n)) * 2 + c, (j // 2) % n, j % 2, slice(None), lanes))], 4 * n, block)
        elif i == 1:
            add_blocks(self.r2a, [(self.r1, lambda j: (x, j // 2, j % 2, first))], 2 * n, lambda j: (j // 2, j % 2))
            add_blocks(self.r2b, [(self.r1, lambda j: (j // n, j % n, y, last))], 2 * n, lambda j: (j // n, j % n))
        elif i == 2:
            add_blocks(self.r3a, [(self.r2a, lambda j: (j, y))], n, lambda j: (j,))
            add_blocks(self.r3b, [(self.r2b, lambda j: (x, j))], n, lambda j: (j,))
        else:
            for ref, slots, rows in ((self.r3a, self.r4a, first), (self.r3b, self.r4b, last)):
                total = ref[place.z].astype(F32)
                for k in range(n - 1):
                    total = total + slots[k].astype(F32)
                self.out[rows, lanes] = total
        if i < 3:
            begin(self.stages[i + 1])

    def finish(self):
        sent(*self.stages)


def scatter_buffers(seq, rows, cols):
    n, half = seq // 2, rows // 2
    return [
        pltpu.VMEM(shape + (cols,), BF)
        for shape in ((2, n, 2, rows), (n, 2, half), (2, n, half), (n, half), (n, half), (n - 1, half), (n - 1, half))
    ]


class Scan:
    def __init__(self, place, reverse, out, inn, box, planes, send, recv):
        self.place, self.reverse = place, reverse
        self.out, self.inn, self.planes = out, inn, planes
        self.pair, self.chip, self.box, self.back = box
        self.chips = HEADS // 2
        self.mine = place.y * 2 + place.x
        self.half, self.rest = place.c * self.chips, (1 - place.c) * self.chips
        self.sems = Semaphores(send, recv)
        other = place.device(c=1 - place.c)
        at = lambda ref, first: ref.at[pl.ds(first, self.chips)]
        near = [lax.rem(self.mine + k, self.chips) for k in range(1, self.chips)]
        chip = lambda m: place.device(y=m // 2, x=m % 2)
        total = planes.at[place.z]
        copy = self.sems.copy
        self.ways = [
            [copy(at(out, self.rest), self.pair, other)],
            [copy(self.chip.at[m], self.box.at[self.mine], chip(m)) for m in near],
            [copy(total, total, place.device(z=place.around(k))) for k in range(1, place.depth)],
            [copy(self.box.at[m], self.back.at[self.mine], chip(m)) for m in near],
            [copy(self.pair, at(inn, self.half), other)],
        ]

    def start(self):
        begin(self.ways[0])

    def chain(self, ref, count):
        kept = iota((STATE_ROWS, 2 * FEATS), 0) != DECAY
        state = jnp.where(kept, 0.0, 1.0)
        for i in range(count):
            d = count - 1 - i if self.reverse else i
            term = ref[d]
            ref[d] = state
            state = state * term[DECAY : DECAY + 1, :] + jnp.where(kept, term, 0.0)
        return state

    def earlier_is_mine(self):
        return (self.place.c == 0) != self.reverse

    def cores(self):
        arrived(self.ways[0])
        kept = iota((STATE_ROWS, 2 * FEATS), 0) != DECAY
        first = jnp.broadcast_to(self.earlier_is_mine(), kept.shape)
        for i in range(self.chips):
            mine, its = self.out[self.half + i], self.pair[i]
            early, late = jnp.where(first, mine, its), jnp.where(first, its, mine)
            self.chip[i] = early * late[DECAY : DECAY + 1, :] + jnp.where(kept, late, 0.0)
        begin(self.ways[1])
        self.box[self.mine] = self.chip[self.mine]

    def plane(self):
        arrived(self.ways[1])
        self.planes[self.place.z] = self.chain(self.box, self.chips)
        begin(self.ways[2])

    def line(self):
        arrived(self.ways[2])
        sent(self.ways[2])
        self.chain(self.planes, self.place.depth)
        before = self.planes[self.place.z]
        for m in range(self.chips):
            own = self.box[m]
            self.box[m] = own + own[DECAY : DECAY + 1, :] * before
        begin(self.ways[3])
        self.back[self.mine] = self.box[self.mine]

    def share(self):
        arrived(self.ways[3])
        sent(self.ways[0])
        first = jnp.broadcast_to(self.earlier_is_mine(), (STATE_ROWS, 2 * FEATS))
        for i in range(self.chips):
            mine, its, before = self.out[self.half + i], self.pair[i], self.back[i]
            early = jnp.where(first, mine, its)
            late = before * early[DECAY : DECAY + 1, :] + early
            self.inn[self.half + i] = jnp.where(first, before, late)
            self.pair[i] = jnp.where(first, late, before)
        begin(self.ways[4])

    def receive(self):
        arrived(self.ways[4])

    def finish(self):
        sent(self.ways[1], self.ways[3], self.ways[4])


class Lines:
    def __init__(self, place, lines, out, buf, sems):
        self.place, self.lines, self.out = place, lines, out
        self.l1, self.l2, self.l3, self.l4 = buf
        z, y, x, c, copy = place.z, place.y, place.x, place.c, sems.copy
        around = range(1, place.depth)
        self.stages = [
            [copy(lines.at[i * 2 + 1 - c], self.l1.at[i], place.device(c=1 - c)) for i in range(2)],
            [copy(self.l1.at[1 - x], self.l2, place.device(x=1 - x))],
            [copy(self.l2, self.l3, place.device(y=1 - y))],
            [copy(self.l3.at[place.around(k)], self.l4.at[k - 1], place.device(z=place.around(k))) for k in around],
        ]

    def start(self):
        begin(self.stages[0])

    def step(self, i):
        place = self.place
        arrived(self.stages[i])
        if i == 0:
            for j in range(2):
                self.l1[j] += self.lines[j * 2 + place.c]
        elif i == 1:
            self.l2[...] += self.l1[place.x]
        elif i == 2:
            self.l3[...] += self.l2[...]
        else:
            total = self.l3[place.z]
            for k in range(place.depth - 1):
                total = total + self.l4[k]
            self.out[...] = total
        if i < 3:
            begin(self.stages[i + 1])

    def finish(self):
        sent(*self.stages)


LINES_COPIES = 2 + 1 + 1 + 3


def greet(place):
    x, y = 1 - place.x, 1 - place.y
    near = [place.device(c=1 - place.c), place.device(x=x), place.device(y=y), place.device(x=x, y=y)]
    near += [place.device(z=place.around(k)) for k in range(1, place.depth)]
    barrier = pltpu.get_barrier_semaphore()
    for device in near:
        pl.semaphore_signal(barrier, inc=1, device_id=device, device_id_type=MESH)
    return lambda: pl.semaphore_wait(barrier, len(near))


def pack(place, r, key, value, query, gate, vectors, bias, up, out, down):
    at = (place.x * 2 + place.c, place.z, place.y)
    rows, ff = key.shape[0], up.shape[1]
    r.gf[at + (slice(None), slice(LANES + ff, None))] = up[...]
    r.gf[at + (slice(None), slice(0, LANES))] = out[...]
    r.gf[at + (slice(None), slice(LANES, LANES + ff))] = down[...]
    r.ga[at + (slice(None), KEY)] = key[...]
    r.ga[at + (slice(None), VALUE)] = value[...]
    r.ga[at + (slice(None), QUERY)] = query[...]
    lines = [gate[...].astype(F32)] + [v[...].astype(F32) for v in vectors]
    lines = jnp.concatenate(lines + [jnp.zeros((10, rows), F32)], axis=0).astype(BF)
    spread = jnp.where(iota((16, LANES), 0) == iota((16, LANES), 1), 1.0, 0.0).astype(BF)
    small = tn(lines, spread)
    lane = iota((rows, LANES), 1)
    for j in range(2):
        left = jnp.full((rows, LANES), bias[j], F32)
        for k in range(3):
            piece = left.astype(BF).astype(F32)
            small = jnp.where(lane == 6 + 3 * j + k, piece, small)
            left = left - piece
    r.ga[at + (slice(None), SMALL)] = small.astype(BF)


def unpack_kernel(half, grad_a, grad_f, lines, result, gtok, *outs):
    out = dict(zip(OUTPUTS, outs))
    rows = grad_a.shape[0]
    ff = (grad_f.shape[1] - LANES) // 2
    out["result"][...] = result[...]
    out["tokens"][...] = gtok[...]
    for i, name in enumerate(("key", "value", "query")):
        out[name][...] = grad_a[:, i * LANES : (i + 1) * LANES]
    out["up"][...] = grad_f[:, LANES + ff :]
    out["out"][...] = grad_f[:, :LANES]
    out["down"][...] = grad_f[:, LANES : LANES + ff]
    own = jnp.where(half == 0, lines[:, :rows], lines[:, rows : 2 * rows])
    for i, name in enumerate(("norm_gain", "norm_shift", "ffn_gain", "ffn_shift")):
        out[name][...] = own[2 + i : 3 + i, :]
    out["gate"][...] = own[0:2, :]
    out["bias"][...] = lines[6:8, 0:1]


OUTPUTS = ("result", "tokens", "norm_gain", "norm_shift", "query", "key", "value", "gate", "bias", "out", "ffn_gain",
           "ffn_shift", "up", "down")


def layer_kernel(names, tokens_all, T, lengths, seed, bias, tok, cot, key, value, query, gate, *given):
    vectors, (up, out, down), given = given[0:4], given[4:7], given[7:]
    (result, gtok, grad_a, grad_f, grad_lines), scratch = given[:5], given[5:]
    place = Place()
    base = place.me * T
    arrays = dict(zip(names, scratch))
    arrays.update({name: arrays[other] for name, other in SHARED.items()})
    scratch = scratch[len(names) :]
    r = Refs(lengths=lengths, seed=seed, tok=tok, cot=cot, result=result, gtok=gtok, xhat=gtok, **arrays)
    sums, scratch = [scratch[7 * i : 7 * i + 7] for i in range(4)], scratch[28:]
    boxes, planes, line_box, sems = (scratch[0:4], scratch[4:8]), scratch[8:10], scratch[10:14], scratch[14:]
    meet = greet(place)
    pack(place, r, key, value, query, gate, vectors, bias, up, out, down)
    gather = Gather(place, r.ga, r.gf, Semaphores(sems[0], sems[1]))
    forth = Scan(place, False, r.out, r.inn, boxes[0], planes[0], sems[2], sems[3])
    home = Scan(place, True, r.adj, r.aend, boxes[1], planes[1], sems[4], sems[5])
    later = Semaphores(sems[6], sems[7])
    up, down = feed_columns(r)
    sum_u = Scatter(place, r.ggf, up, grad_f, sums[0], later)
    sum_d = Scatter(place, r.ggf, slice(0, down.stop), grad_f, sums[1], later)
    sum_q = Scatter(place, r.gga, slice(2 * LANES, 3 * LANES), grad_a, sums[2], later)
    sum_k = Scatter(place, r.gga, slice(0, 2 * LANES), grad_a, sums[3], later)
    lines = Lines(place, r.lines, grad_lines, line_box, later)
    meet()

    g = gather.step
    others_first = lambda i: (i % 2) * 2 + jnp.where(i < 2, 1 - place.c, place.c)
    gather.begin(0)
    tables(T, base, r)
    g(0, 0)
    gather.begin(1)
    g(0, 1)
    g(1, 0)
    gather.begin(2)
    g(0, 2)
    g(1, 1)
    g(0, 3)
    first_norm(T, base, r)
    g(2, 0)
    gather.begin(3)
    keys(T, base, r, {0: [(g, 1, 2)], 3: [(g, 2, 1), (g, 1, 3)]})
    states(T, base, r)
    forth.start()
    queries(T, base, r, {0: [(forth.cores,)], 1: [(g, 3, 0)], 2: [(forth.plane,)], 3: [(g, 2, 2), (g, 3, 1)]})
    g(2, 3)
    cotangents(T, base, r)
    forth.line()
    g(3, 2)
    forth.share()
    g(3, 3)
    forth.receive()
    forth.finish()
    attend(T, base, r)
    feed(T, base, r)
    home.start()
    up_grads(T, base, r)
    sum_u.start()
    home.cores()
    down_grads(T, base, r)
    sum_d.start()
    near = {0: [(home.plane,), (sum_u.step, 0)], 1: [(sum_d.step, 0)], 2: [(home.line,)],
            3: [(sum_q.start,), (sum_u.step, 1), (home.share,)]}
    far = {0: [(sum_q.step, 0), (sum_d.step, 1)], 1: [(sum_k.start,), (sum_u.step, 2)], 2: [(sum_q.step, 1)],
           3: [(sum_k.step, 0)]}
    back(T, base, r, tokens_all, near, home.receive, far, others_first)
    lines.start()
    sum_q.step(2)
    sum_d.step(2)
    sum_k.step(1)
    lines.step(0)
    sum_u.step(3)
    lines.step(1)
    sum_k.step(2)
    lines.step(2)
    sum_q.step(3)
    sum_d.step(3)
    sum_k.step(3)
    lines.step(3)
    gather.finish()
    home.finish()
    for each in (sum_u, sum_d, sum_q, sum_k, lines):
        each.finish()


def layer_near(lengths, seed, tokens, cotangent, weights, specs, seq, head):
    T, D = tokens.shape
    count = seq * head
    rows, ff = D // seq, specs["act"][0][2]
    held = [n for n in dict.fromkeys(sum((sum(names, ()) for names in (FRONT, MIDDLE, BACK)), ())) if n not in SHARED]
    held = [n for n in held if n not in ("result", "gtok", "xhat")]
    dma = pltpu.SemaphoreType.DMA
    scratch = [pltpu.VMEM(*specs[n]) for n in held]
    panels = 3 * LANES
    widths = (ff, LANES + ff, LANES, 2 * LANES)
    states = lambda count: pltpu.VMEM((count,) + STATES[1:], F32)
    for width in widths:
        scratch += scatter_buffers(seq, rows, width)
    scratch += [states(HEADS // 2)] * 8 + [states(seq // 2)] * 2
    tiles = lambda *lead: pltpu.VMEM(lead + (8, LANES), F32)
    scratch += [tiles(2, D // LANES), tiles(D // LANES), tiles(D // LANES), tiles(seq // 2 - 1)]
    scratch += [dma((4 * GATHER_COPIES,))] * 2 + [dma((16,))] * 4 + [dma((4 * SCATTER_COPIES + LINES_COPIES,))] * 2
    vmem, smem = pl.BlockSpec(memory_space=pltpu.VMEM), pl.BlockSpec(memory_space=pltpu.SMEM)
    shape = jax.ShapeDtypeStruct
    result, gtok, grad_a, grad_f, lines = pl.pallas_call(
        functools.partial(layer_kernel, held, T * count, T),
        out_shape=[shape((T, D), BF), shape((T, D), F32), shape((rows, panels), F32), shape((rows, 2 * ff + LANES), F32),
                   shape((8, LANES), F32)],
        in_specs=[smem] * 3 + [vmem] * 13,
        out_specs=[vmem] * 5,
        scratch_shapes=scratch,
        compiler_params=pltpu.CompilerParams(collective_id=0, has_side_effects=True, vmem_limit_bytes=LAYER_BYTES),
        name="layer",
    )(lengths, seed, weights[0], tokens, cotangent, *weights[1:])
    line, square = shape((1, rows), F32), shape((rows, LANES), F32)
    shapes = (shape((T, D), BF), shape((T, D), F32), line, line, square, square, square, shape((2, rows), F32),
              shape((2, 1), F32), square, line, line, shape((rows, ff), F32), shape((rows, ff), F32))

    def unpacked(*refs):
        unpack_kernel(lax.axis_index("seq") % 2, *refs)

    outs = pl.pallas_call(
        unpacked,
        out_shape=shapes,
        in_specs=[vmem] * 5,
        out_specs=[vmem] * len(shapes),
        compiler_params=pltpu.CompilerParams(vmem_limit_bytes=VMEM_BYTES),
        name="unpack",
    )(grad_a, grad_f, lines, result, gtok)
    flat = ("norm_gain", "norm_shift", "bias", "ffn_gain", "ffn_shift")
    turned = ("gate", "out", "down")
    return tuple(x.reshape(-1) if n in flat else x.T if n in turned else x for n, x in zip(OUTPUTS, outs))


def bias_columns(gate_bias):
    hi = lax.reduce_precision(gate_bias, 8, 7)
    mid = lax.reduce_precision(gate_bias - hi, 8, 7)
    return jnp.stack([hi, mid, gate_bias - hi - mid], axis=1).astype(BF)


def gather_any(q, k, v, gate, vectors, bias, out, up, down, seq):
    D = q.shape[0] * seq

    def whole(w, rows, cols):
        w = lax.all_gather(w, rows, axis=0, tiled=True)
        return lax.all_gather(w, cols, axis=1, tiled=True)

    def panels(w):
        return w.reshape(D, PAIRS, w.shape[1] // PAIRS).transpose(1, 0, 2)

    q, k, v = (panels(whole(w, "seq", "head")) for w in (q, k, v))
    gates = panels(whole(gate, "seq", "head"))
    lines = [jnp.broadcast_to(lax.all_gather(w, "seq", tiled=True)[None, :, None], (PAIRS, D, 1)) for w in vectors]
    bias = bias_columns(lax.all_gather(bias, "head", tiled=True)).reshape(PAIRS, 1, 6)
    pad = jnp.zeros((PAIRS, D, LANES - 12), BF)
    ga = jnp.concatenate([k, gates] + lines + [jnp.broadcast_to(bias, (PAIRS, D, 6)), pad, v, q], axis=2)
    gf = [panels(whole(out, "head", "seq").T), panels(whole(down, "head", "seq").T), panels(whole(up, "seq", "head"))]
    gf = jnp.concatenate(gf, axis=2)
    shape = (PAIRS, seq // 2, 2, D // seq)
    return ga.reshape(shape + ga.shape[2:]), gf.reshape(shape + gf.shape[2:])


def scatter_any(gga, ggf, lines, ff):
    gga, ggf = (x.reshape(PAIRS, -1, x.shape[-1]).astype(F32) for x in (gga, ggf))

    def grid(x):
        x = x.transpose(1, 0, 2).reshape(x.shape[1], -1)
        x = lax.psum_scatter(x, "seq", scatter_dimension=0, tiled=True)
        return lax.psum_scatter(x, "head", scatter_dimension=1, tiled=True)

    block = lambda i: gga[:, :, i * LANES : (i + 1) * LANES]
    lines = lines.transpose(0, 2, 1, 3).reshape(PAIRS, 8, -1)
    gates = lines[:, 0:2].transpose(0, 2, 1)
    bias = lines[:, 6:8, 0].reshape(HEADS)
    bias = lax.psum_scatter(lax.psum(bias, "seq"), "head", scatter_dimension=0, tiled=True)
    lines = lax.psum_scatter(lax.psum(lines[0, 2:6].T, "head"), "seq", scatter_dimension=0, tiled=True)
    return (
        lines[:, 0], lines[:, 1], grid(block(2)), grid(block(0)), grid(block(1)), grid(gates), bias,
        grid(ggf[:, :, :LANES]).T, lines[:, 2], lines[:, 3], grid(ggf[:, :, LANES + ff :]),
        grid(ggf[:, :, LANES : LANES + ff]).T,
    )


def shards(
    tokens, lengths, feature_seed, norm_gain, norm_shift, query_weight, key_weight, value_weight, gate_weight, gate_bias,
    out_weight, ffn_gain, ffn_shift, up_weight, down_weight, cotangent,
):
    seq, head = lax.axis_size("seq"), lax.axis_size("head")
    T, D = tokens.shape
    rows = D // seq
    ff = up_weight.shape[1] * head // PAIRS
    vectors = (norm_gain, norm_shift, ffn_gain, ffn_shift)
    specs = buffers(T, D, ATT, LANES + 2 * ff, ff, seq)
    if (seq, head) == (HEADS, PAIRS):
        weights = (gate_bias, key_weight, value_weight, query_weight, gate_weight.T)
        weights += tuple(w.reshape(1, rows) for w in vectors) + (up_weight, out_weight.T, down_weight.T)
        return layer_near(lengths, feature_seed, tokens, cotangent, weights, specs, seq, head)
    ga, gf = gather_any(query_weight, key_weight, value_weight, gate_weight, vectors, gate_bias, out_weight, up_weight,
                        down_weight, seq)
    args = (here(T).astype(I32).reshape(1), lengths, feature_seed, tokens, cotangent)
    state = {"ga": ga, "gf": gf}
    stage(lambda base, r: front(T, base, r), FRONT, specs, "front", args, state)
    state["inn"] = scan_states(state["out"], False)
    stage(lambda base, r: middle(T, base, r), MIDDLE, specs, "middle", args, state)
    state["aend"] = scan_states(state["adj"], True)
    stage(lambda base, r: back(T, base, r, T * seq * head), BACK, specs, "back", args, state)
    return (state["result"], state["gtok"]) + scatter_any(state["gga"], state["ggf"], state["lines"], ff)


def solution(mesh):
    both, rows, grid = P(("seq", "head"), None), P("seq"), P("seq", "head")
    return jax.shard_map(
        shards,
        mesh=mesh,
        in_specs=(both, P(), P(), rows, rows, grid, grid, grid, grid, P("head"), P("head", "seq"), rows, rows, grid,
                  P("head", "seq"), both),
        out_specs=(both, both, rows, rows, grid, grid, grid, grid, P("head"), P("head", "seq"), rows, rows, grid,
                   P("head", "seq")),
        check_vma=False,
    )
```

profile of v0, /device:TPU:0, one launch (start us, length us, event | category | flops | bytes accessed | tf_op | source)
XLA Modules:
  0.0 132.6 jit_solution(2418692788564696930)
XLA Ops:
  1.3 127.2 %layer.1 = (bf16[512,512]{1,0:T(8,128)(2,1)}, f32[512,512]{1,0:T(8,128)}, f32[64,384]{1,0:T(8,128)}, f32[64,1152]{1,0:T(8,128)}, f32[8,128]{1,0:T(8,128)}) custom-call(s32[3]{0:T(128)} %lengths.1, s32[1]{0:T(128)S(6)} %copy.30.seed, f32[2]{0:T(128)} %bias.1, bf16[512,512]{1,0:T(8,128)(2,1)} %tok.1, bf16[512,512]{1,0:T(8,128)(2,1)} %cot.1, ...), custom_call_target="tpu_custom_call" | custom-call | tf_op jit(solution)/shard_map/layer/pallas_call | solution.py:1164
  128.5 2.8 %unpack.1 = (bf16[512,512]{1,0:T(8,128)(2,1)}, f32[512,512]{1,0:T(8,128)}, f32[1,64]{1,0:T(1,128)}, f32[1,64]{1,0:T(1,128)}, f32[64,128]{1,0:T(8,128)}, /*index=...) custom-call(f32[64,384]{1,0:T(8,128)} %get-tuple-element.33.refs_0_,, ...), custom_call_target="tpu_custom_call" | custom-call | tf_op jit(solution)/shard_map/unpack/pallas_call | solution.py:1181
  131.4 0.0 copy-start
  131.4 0.6 copy-done
  132.0 0.6 reduce
Async XLA Ops:
  131.4 0.6 copy-start
where the time goes:
time: 133 us
  Pallas kernels  130 us (98%)
    pallas_call x1, Pallas kernels, layer_near(): pl.pallas_call(functools.partial(layer_kernel, held, T * count, T), out_s...  127 us
    pallas_call x1, Pallas kernels, layer_near(): pl.pallas_call(unpacked, out_shape=shapes, in_specs=[vmem] * 5, out_specs...  2.85 us

commit v1 on v0

--- a/solution.py
+++ b/solution.py
@@ -22,8 +22,8 @@
 COS = (0.9999992193982472, -0.4999942543676011, 0.04165980908449851, -0.0013858873219640337,
        2.420384320646774e-05, -2.1976364824224383e-07)
 ERFC = (0.254829592, -0.284496736, 1.421413741, -1.453152027, 1.061405429)
-ATT = 4 * LANES
-KEY, SMALL, VALUE, QUERY = (slice(i * LANES, (i + 1) * LANES) for i in range(4))
+ATT = 3 * LANES
+KEY, VALUE, QUERY = (slice(i * LANES, (i + 1) * LANES) for i in range(3))
 NORMAL, DECAY, STATE_ROWS = HEAD_DIM, HEAD_DIM + 1, HEAD_DIM + 8
 STATES = (HEADS, STATE_ROWS, 2 * FEATS)
 VMEM_BYTES = 56 * 1024 * 1024
@@ -207,9 +207,8 @@
 
 
 def first_norm(T, base, r):
-    pick = jnp.where(iota((16, LANES), 0) == iota((16, LANES), 1), 1.0, 0.0).astype(BF)
     for p in range(PAIRS):
-        rows = nt(pick, panel(r.ga, p, SMALL))
+        rows = r.small[p]
         r.gate[2 * p : 2 * p + 2, :] = rows[0:2]
         r.gate[8 + 2 * p : 10 + 2 * p, :] = rows[0:2]
         r.bias[2 * p : 2 * p + 1, :] = rows[6:7] + rows[7:8] + rows[8:9]
@@ -544,8 +543,7 @@
             r.owed[pl.ds(h, 1), :] = jnp.broadcast_to(owed, (1, LANES))
         grad_v = jnp.where(low, grad_v[0], grad_v[1]).astype(BF)
         grads = jnp.concatenate([feature_back(p, r.k[p], r.da[p, :, 2 * FEATS :]), grad_v], axis=1)
-        weights = jnp.concatenate([panel(r.ga, p, KEY), panel(r.ga, p, VALUE)], axis=1)
-        r.acc1[...] += nt(grads, weights)
+        r.acc1[...] += nt(grads, panel(r.ga, p, slice(0, 2 * LANES)))
         put_panel(r.gga, p, slice(0, 2 * LANES), tn(r.normed[...], grads))
 
     run_pairs(near, near_hook, order)
@@ -600,7 +598,7 @@
     z = (PAIRS, seq // 2, 2, D // seq)
     pair = (PAIRS, T, LANES)
     return {
-        "ga": (z + (att,), BF), "gf": (z + (rest,), BF), "gga": (z + (att - LANES,), BF), "ggf": (z + (rest,), BF),
+        "ga": (z + (att,), BF), "gf": (z + (rest,), BF), "gga": (z + (att,), BF), "small": ((PAIRS, 16, D), F32), "ggf": (z + (rest,), BF),
         "gate": ((16, D), F32), "bias": ((8, D), F32), "vec": ((8, D), F32), "normed": ((T, D), BF),
         "logits": ((8, T), F32), "run": ((8, T), F32), "total": ((8, LANES), F32), "mask": ((T, T), F32),
         "s1": ((T, 2 * FEATS), F32), "s2": ((T, 2 * FEATS), F32), "s": ((T, T), F32),
@@ -620,7 +618,7 @@
 
 
 FRONT = (
-    ("ga",),
+    ("ga", "small"),
     ("gate", "vec", "normed", "logits", "run", "total", "mask", "tabn", "q", "k", "v", "rb", "qf", "kf", "out", "w", "own", "zfix"),
     ("bias", "s1", "s2", "s", "tab"),
 )
@@ -778,18 +776,25 @@
 
 
 class Gather:
-    def __init__(self, place, ga, gf, sems):
+    def __init__(self, place, ga, gf, gs, sems):
         ff = (gf.shape[-1] - LANES) // 2
         lanes = lambda first, count: pl.ds(first, count)
         self.chunks = [
             gather_stages(place, ref, part, sems)
             for ref, part in (
-                (ga, lanes(0, 2 * LANES)),
-                (ga, lanes(2 * LANES, 2 * LANES)),
+                (ga, lanes(0, LANES)),
+                (ga, lanes(LANES, 2 * LANES)),
                 (gf, lanes(0, LANES + ff)),
                 (gf, lanes(LANES + ff, ff)),
             )
         ]
+
+        z, y, x, c, pair = place.z, place.y, place.x, place.c, place.x * 2 + place.c
+        first, same = self.chunks[0], lambda ref, **to: sems.copy(ref, ref, place.device(**to))
+        first[0] += [same(gs.at[pair, z, y], z=place.around(k)) for k in range(1, place.depth)]
+        first[1].append(same(gs.at[pair, :, y], y=1 - y))
+        first[2].append(same(gs.at[pair], x=1 - x))
+        first[3] += [same(gs.at[other * 2 + c], c=1 - c) for other in range(2)]
 
     def begin(self, chunk):
         begin(self.chunks[chunk][0])
@@ -1023,17 +1028,23 @@
     r.ga[at + (slice(None), VALUE)] = value[...]
     r.ga[at + (slice(None), QUERY)] = query[...]
     lines = [gate[...].astype(F32)] + [v[...].astype(F32) for v in vectors]
-    lines = jnp.concatenate(lines + [jnp.zeros((10, rows), F32)], axis=0).astype(BF)
-    spread = jnp.where(iota((16, LANES), 0) == iota((16, LANES), 1), 1.0, 0.0).astype(BF)
-    small = tn(lines, spread)
-    lane = iota((rows, LANES), 1)
     for j in range(2):
-        left = jnp.full((rows, LANES), bias[j], F32)
-        for k in range(3):
+        left = jnp.full((1, rows), bias[j], F32)
+        for _ in range(3):
             piece = left.astype(BF).astype(F32)
-            small = jnp.where(lane == 6 + 3 * j + k, piece, small)
+            lines.append(piece)
             left = left - piece
-    r.ga[at + (slice(None), SMALL)] = small.astype(BF)
+    lines = jnp.concatenate(lines + [jnp.zeros((4, rows), F32)], axis=0).astype(BF)
+    wide = jnp.where(iota((rows, LANES), 0) == iota((rows, LANES), 1), 1.0, 0.0).astype(BF)
+    r.gs[at] = nn(lines, wide).astype(BF)
+
+
+def spread_small(r):
+    for p in range(PAIRS):
+        for z in range(r.gs.shape[1]):
+            even, odd = r.gs[p, z, 0].astype(F32), r.gs[p, z, 1].astype(F32)
+            tile = jnp.where(low_lanes(16), even, pltpu.roll(odd, HEAD_DIM, 1))
+            r.small[p, :, z * LANES : (z + 1) * LANES] = tile
 
 
 def unpack_kernel(half, grad_a, grad_f, lines, result, gtok, *outs):
@@ -1051,16 +1062,21 @@
     for i, name in enumerate(("norm_gain", "norm_shift", "ffn_gain", "ffn_shift")):
         out[name][...] = own[2 + i : 3 + i, :]
     out["gate"][...] = own[0:2, :]
-    out["bias"][...] = lines[6:8, 0:1]
+    out["bias"][...] = jnp.where(iota((1, LANES), 1) == 0, lines[6:7, :], lines[7:8, :])[:, 0:2]
 
 
 OUTPUTS = ("result", "tokens", "norm_gain", "norm_shift", "query", "key", "value", "gate", "bias", "out", "ffn_gain",
            "ffn_shift", "up", "down")
 
 
-def layer_kernel(names, tokens_all, T, lengths, seed, bias, tok, cot, key, value, query, gate, *given):
+def layer_kernel(names, tokens_all, T, lengths, seed, bias, tok_in, cot_in, key, value, query, gate, *given):
     vectors, (up, out, down), given = given[0:4], given[4:7], given[7:]
-    (result, gtok, grad_a, grad_f, grad_lines), scratch = given[:5], given[5:]
+    (result_out, gtok_out, grad_a, grad_f, grad_lines), scratch = given[:5], given[5:]
+    (tok, cot, result, gtok, moves), scratch = scratch[:5], scratch[5:]
+    moves = [pltpu.make_async_copy(src, dst, moves.at[i]) for i, (src, dst) in enumerate(
+        ((tok_in, tok), (cot_in, cot), (result, result_out), (gtok, gtok_out)))]
+    moves[0].start()
+    moves[1].start()
     place = Place()
     base = place.me * T
     arrays = dict(zip(names, scratch))
@@ -1071,7 +1087,7 @@
     boxes, planes, line_box, sems = (scratch[0:4], scratch[4:8]), scratch[8:10], scratch[10:14], scratch[14:]
     meet = greet(place)
     pack(place, r, key, value, query, gate, vectors, bias, up, out, down)
-    gather = Gather(place, r.ga, r.gf, Semaphores(sems[0], sems[1]))
+    gather = Gather(place, r.ga, r.gf, r.gs, Semaphores(sems[0], sems[1]))
     forth = Scan(place, False, r.out, r.inn, boxes[0], planes[0], sems[2], sems[3])
     home = Scan(place, True, r.adj, r.aend, boxes[1], planes[1], sems[4], sems[5])
     later = Semaphores(sems[6], sems[7])
@@ -1095,6 +1111,8 @@
     g(0, 2)
     g(1, 1)
     g(0, 3)
+    spread_small(r)
+    moves[0].wait()
     first_norm(T, base, r)
     g(2, 0)
     gather.begin(3)
@@ -1103,6 +1121,7 @@
     forth.start()
     queries(T, base, r, {0: [(forth.cores,)], 1: [(g, 3, 0)], 2: [(forth.plane,)], 3: [(g, 2, 2), (g, 3, 1)]})
     g(2, 3)
+    moves[1].wait()
     cotangents(T, base, r)
     forth.line()
     g(3, 2)
@@ -1113,16 +1132,18 @@
     attend(T, base, r)
     feed(T, base, r)
     home.start()
+    moves[2].start()
     up_grads(T, base, r)
     sum_u.start()
     home.cores()
     down_grads(T, base, r)
     sum_d.start()
-    near = {0: [(home.plane,), (sum_u.step, 0)], 1: [(sum_d.step, 0)], 2: [(home.line,)],
-            3: [(sum_q.start,), (sum_u.step, 1), (home.share,)]}
-    far = {0: [(sum_q.step, 0), (sum_d.step, 1)], 1: [(sum_k.start,), (sum_u.step, 2)], 2: [(sum_q.step, 1)],
+    near = {0: [(home.plane,), (sum_u.step, 0)], 2: [(home.line,)],
+            3: [(sum_u.step, 1), (sum_q.start,), (home.share,), (sum_d.step, 0)]}
+    far = {0: [(sum_q.step, 0)], 1: [(sum_k.start,), (sum_u.step, 2)], 2: [(sum_d.step, 1), (sum_q.step, 1)],
            3: [(sum_k.step, 0)]}
     back(T, base, r, tokens_all, near, home.receive, far, others_first)
+    moves[3].start()
     lines.start()
     sum_q.step(2)
     sum_d.step(2)
@@ -1138,6 +1159,8 @@
     lines.step(3)
     gather.finish()
     home.finish()
+    moves[2].wait()
+    moves[3].wait()
     for each in (sum_u, sum_d, sum_q, sum_k, lines):
         each.finish()
 
@@ -1149,7 +1172,11 @@
     held = [n for n in dict.fromkeys(sum((sum(names, ()) for names in (FRONT, MIDDLE, BACK)), ())) if n not in SHARED]
     held = [n for n in held if n not in ("result", "gtok", "xhat")]
     dma = pltpu.SemaphoreType.DMA
-    scratch = [pltpu.VMEM(*specs[n]) for n in held]
+    specs = dict(specs, gs=((PAIRS, seq // 2, 2, 16, LANES), BF))
+    held.append("gs")
+    wide = lambda kind: pltpu.VMEM((T, D), kind)
+    scratch = [wide(BF), wide(BF), wide(BF), wide(F32), dma((4,))]
+    scratch += [pltpu.VMEM(*specs[n]) for n in held]
     panels = 3 * LANES
     widths = (ff, LANES + ff, LANES, 2 * LANES)
     states = lambda count: pltpu.VMEM((count,) + STATES[1:], F32)
@@ -1158,22 +1185,22 @@
     scratch += [states(HEADS // 2)] * 8 + [states(seq // 2)] * 2
     tiles = lambda *lead: pltpu.VMEM(lead + (8, LANES), F32)
     scratch += [tiles(2, D // LANES), tiles(D // LANES), tiles(D // LANES), tiles(seq // 2 - 1)]
-    scratch += [dma((4 * GATHER_COPIES,))] * 2 + [dma((16,))] * 4 + [dma((4 * SCATTER_COPIES + LINES_COPIES,))] * 2
+    scratch += [dma((5 * GATHER_COPIES,))] * 2 + [dma((16,))] * 4 + [dma((4 * SCATTER_COPIES + LINES_COPIES,))] * 2
     vmem, smem = pl.BlockSpec(memory_space=pltpu.VMEM), pl.BlockSpec(memory_space=pltpu.SMEM)
-    shape = jax.ShapeDtypeStruct
+    shape, far = jax.ShapeDtypeStruct, pl.BlockSpec(memory_space=pl.ANY)
     result, gtok, grad_a, grad_f, lines = pl.pallas_call(
         functools.partial(layer_kernel, held, T * count, T),
         out_shape=[shape((T, D), BF), shape((T, D), F32), shape((rows, panels), F32), shape((rows, 2 * ff + LANES), F32),
                    shape((8, LANES), F32)],
-        in_specs=[smem] * 3 + [vmem] * 13,
-        out_specs=[vmem] * 5,
+        in_specs=[smem] * 3 + [far] * 2 + [vmem] * 11,
+        out_specs=[far] * 2 + [vmem] * 3,
         scratch_shapes=scratch,
         compiler_params=pltpu.CompilerParams(collective_id=0, has_side_effects=True, vmem_limit_bytes=LAYER_BYTES),
         name="layer",
     )(lengths, seed, weights[0], tokens, cotangent, *weights[1:])
     line, square = shape((1, rows), F32), shape((rows, LANES), F32)
     shapes = (shape((T, D), BF), shape((T, D), F32), line, line, square, square, square, shape((2, rows), F32),
-              shape((2, 1), F32), square, line, line, shape((rows, ff), F32), shape((rows, ff), F32))
+              shape((1, 2), F32), square, line, line, shape((rows, ff), F32), shape((rows, ff), F32))
 
     def unpacked(*refs):
         unpack_kernel(lax.axis_index("seq") % 2, *refs)
@@ -1211,12 +1238,14 @@
     gates = panels(whole(gate, "seq", "head"))
     lines = [jnp.broadcast_to(lax.all_gather(w, "seq", tiled=True)[None, :, None], (PAIRS, D, 1)) for w in vectors]
     bias = bias_columns(lax.all_gather(bias, "head", tiled=True)).reshape(PAIRS, 1, 6)
-    pad = jnp.zeros((PAIRS, D, LANES - 12), BF)
-    ga = jnp.concatenate([k, gates] + lines + [jnp.broadcast_to(bias, (PAIRS, D, 6)), pad, v, q], axis=2)
+    ga = jnp.concatenate([k, v, q], axis=2)
+    rows = [gates.transpose(0, 2, 1)] + [w.transpose(0, 2, 1) for w in lines]
+    rows += [jnp.broadcast_to(bias.transpose(0, 2, 1), (PAIRS, 6, D)), jnp.zeros((PAIRS, 4, D), BF)]
+    small = jnp.concatenate(rows, axis=1).astype(F32)
     gf = [panels(whole(out, "head", "seq").T), panels(whole(down, "head", "seq").T), panels(whole(up, "seq", "head"))]
     gf = jnp.concatenate(gf, axis=2)
     shape = (PAIRS, seq // 2, 2, D // seq)
-    return ga.reshape(shape + ga.shape[2:]), gf.reshape(shape + gf.shape[2:])
+    return ga.reshape(shape + ga.shape[2:]), gf.reshape(shape + gf.shape[2:]), small
 
 
 def scatter_any(gga, ggf, lines, ff):
@@ -1254,10 +1283,10 @@
         weights = (gate_bias, key_weight, value_weight, query_weight, gate_weight.T)
         weights += tuple(w.reshape(1, rows) for w in vectors) + (up_weight, out_weight.T, down_weight.T)
         return layer_near(lengths, feature_seed, tokens, cotangent, weights, specs, seq, head)
-    ga, gf = gather_any(query_weight, key_weight, value_weight, gate_weight, vectors, gate_bias, out_weight, up_weight,
+    ga, gf, small = gather_any(query_weight, key_weight, value_weight, gate_weight, vectors, gate_bias, out_weight, up_weight,
                         down_weight, seq)
     args = (here(T).astype(I32).reshape(1), lengths, feature_seed, tokens, cotangent)
-    state = {"ga": ga, "gf": gf}
+    state = {"ga": ga, "gf": gf, "small": small}
     stage(lambda base, r: front(T, base, r), FRONT, specs, "front", args, state)
     state["inn"] = scan_states(state["out"], False)
     stage(lambda base, r: middle(T, base, r), MIDDLE, specs, "middle", args, state)

time: 133 us -> 126 us (0.947)
  Pallas kernels: 130 us -> 125 us
    pallas_call x1, Pallas kernels: 127 us -> 122 us  [layer_near(): pl.pallas_call(functools.partial(layer_kernel, held, T * count, T), out_s...]
where the time goes in v1:
time: 126 us
  Pallas kernels  125 us (99%)
  between operations  1.37 us (1%)
    pallas_call x1, Pallas kernels, layer_near(): pl.pallas_call(functools.partial(layer_kernel, held, T * count, T), out_s...  122 us
    pallas_call x1, Pallas kernels, layer_near(): pl.pallas_call(unpacked, out_shape=shapes, in_specs=[vmem] * 5, out_specs...  2.85 us

profile of v1, /device:TPU:0, one launch (start us, length us, event | category | flops | bytes accessed | tf_op | source)
XLA Modules:
  0.0 126.0 jit_solution(9059875373073731555)
XLA Ops:
  1.3 121.8 %layer.1 = (bf16[512,512]{1,0:T(8,128)(2,1)}, f32[512,512]{1,0:T(8,128)}, f32[64,384]{1,0:T(8,128)}, f32[64,1152]{1,0:T(8,128)}, f32[8,128]{1,0:T(8,128)}) custom-call(s32[3]{0:T(128)} %lengths.1, s32[1]{0:T(128)S(6)} %copy.30.seed, f32[2]{0:T(128)} %bias.1, bf16[512,512]{1,0:T(8,128)(2,1)} %tok_in.1, bf16[512,512]{1,0:T(8,128)(2,1)} %cot_in.1, ...), custom_call_target="tpu_custom_call" | custom-call | tf_op jit(solution)/shard_map/layer/pallas_call | solution.py:1191
  123.1 2.8 %unpack.1 = (bf16[512,512]{1,0:T(8,128)(2,1)}, f32[512,512]{1,0:T(8,128)}, f32[1,64]{1,0:T(1,128)}, f32[1,64]{1,0:T(1,128)}, f32[64,128]{1,0:T(8,128)}, /*index=...) custom-call(f32[64,384]{1,0:T(8,128)} %get-tuple-element.33.refs_0_,, ...), custom_call_target="tpu_custom_call" | custom-call | tf_op jit(solution)/shard_map/unpack/pallas_call | solution.py:1208

commit v2 on v1

--- a/solution.py
+++ b/solution.py
@@ -55,12 +55,13 @@
     body(pl.ds(0, total), 0, total)
 
 
-def pair_loop(body):
-    def one(p, carry):
-        body(p)
+def pair_loop(body, straight=1):
+    def one(i, carry):
+        for k in range(straight):
+            body(i * straight + k)
         return carry
 
-    lax.fori_loop(0, PAIRS, one, 0)
+    lax.fori_loop(0, PAIRS // straight, one, 0)
 
 
 def head_ones(rows, cols, row_span, col_span):
@@ -154,7 +155,7 @@
     return jnp.concatenate([x, x], axis=1)
 
 
-def run_pairs(body, hook, order=None):
+def run_pairs(body, hook, order=None, straight=1):
     def one(p):
         body(order(p) if order else p)
         for at, acts in (hook or {}).items():
@@ -164,7 +165,7 @@
                 for act, *given in acts:
                     act(*given)
 
-    pair_loop(one)
+    pair_loop(one, straight)
 
 
 def tables(T, base, r):
@@ -206,6 +207,10 @@
     pair_loop(table)
 
 
+def standardise(T, base, r):
+    r.xhat[...] = norm_stats(r.tok[...].astype(F32))[0]
+
+
 def first_norm(T, base, r):
     for p in range(PAIRS):
         rows = r.small[p]
@@ -216,11 +221,7 @@
         if p == 0:
             r.vec[...] = rows[0:8]
 
-    def norm_rows(rows, at, n):
-        xhat, _ = norm_stats(r.tok[rows, :].astype(F32))
-        r.normed[rows, :] = (xhat * r.vec[2:3, :] + r.vec[3:4, :]).astype(BF)
-
-    rows_loop(T, 64, norm_rows)
+    r.normed[...] = (r.xhat[...] * r.vec[2:3, :] + r.vec[3:4, :]).astype(BF)
     logits = nt(r.gate[...].astype(BF), r.normed[...])[0:8] + r.bias[:, 0:1]
     r.logits[...] = logits
     pos = base + iota((8, T), 1)
@@ -344,7 +345,7 @@
         z = pltpu.roll(jnp.where(low, total[1], total[0]), HEAD_DIM, 1) + r.zfix[p].astype(F32)
         r.att[p] = (live_col * num * lax.rsqrt(z * z + FLOOR2)).astype(BF)
 
-    pair_loop(join)
+    pair_loop(join, 4)
     o = out_columns(r)
     branch = None
     for p in range(0, PAIRS, 2):
@@ -447,7 +448,7 @@
             normal = 0.5 * (adj[at : at + 1] + adj[at + half : at + half + 1])
             put_state(r.adj, h, adj[a * HEAD_DIM : (a + 1) * HEAD_DIM], normal, r.total[pl.ds(h, 1), :])
 
-    pair_loop(back)
+    pair_loop(back, 4)
 
 
 def up_grads(T, base, r):
@@ -620,7 +621,7 @@
 FRONT = (
     ("ga", "small"),
     ("gate", "vec", "normed", "logits", "run", "total", "mask", "tabn", "q", "k", "v", "rb", "qf", "kf", "out", "w", "own", "zfix"),
-    ("bias", "s1", "s2", "s", "tab"),
+    ("bias", "s1", "s2", "s", "tab", "xhat"),
 )
 MIDDLE = (
     ("gf", "vec", "rb", "qf", "own", "zfix", "inn", "total"),
@@ -638,6 +639,7 @@
 
 def front(T, base, r):
     tables(T, base, r)
+    standardise(T, base, r)
     first_norm(T, base, r)
     keys(T, base, r)
     states(T, base, r)
@@ -1110,9 +1112,10 @@
     gather.begin(2)
     g(0, 2)
     g(1, 1)
+    moves[0].wait()
+    standardise(T, base, r)
     g(0, 3)
     spread_small(r)
-    moves[0].wait()
     first_norm(T, base, r)
     g(2, 0)
     gather.begin(3)

time: 126 us -> 124 us (0.984)
  Pallas kernels: 125 us -> 122 us
    pallas_call x1, Pallas kernels: 122 us -> 119 us  [layer_near(): pl.pallas_call(functools.partial(layer_kernel, held, T * count, T), out_s...]
where the time goes in v2:
time: 124 us
  Pallas kernels  122 us (98%)
  between operations  1.37 us (1%)
    pallas_call x1, Pallas kernels, layer_near(): pl.pallas_call(functools.partial(layer_kernel, held, T * count, T), out_s...  119 us
    pallas_call x1, Pallas kernels, layer_near(): pl.pallas_call(unpacked, out_shape=shapes, in_specs=[vmem] * 5, out_specs...  2.85 us

profile of v2, /device:TPU:0, one launch (start us, length us, event | category | flops | bytes accessed | tf_op | source)
XLA Modules:
  0.0 123.6 jit_solution(14095776792384645695)
XLA Ops:
  1.3 119.3 %layer.1 = (bf16[512,512]{1,0:T(8,128)(2,1)}, f32[512,512]{1,0:T(8,128)}, f32[64,384]{1,0:T(8,128)}, f32[64,1152]{1,0:T(8,128)}, f32[8,128]{1,0:T(8,128)}) custom-call(s32[3]{0:T(128)} %lengths.1, s32[1]{0:T(128)S(6)} %copy.30.seed, f32[2]{0:T(128)} %bias.1, bf16[512,512]{1,0:T(8,128)(2,1)} %tok_in.1, bf16[512,512]{1,0:T(8,128)(2,1)} %cot_in.1, ...), custom_call_target="tpu_custom_call" | custom-call | tf_op jit(solution)/shard_map/layer/pallas_call | solution.py:1194
  120.7 2.8 %unpack.1 = (bf16[512,512]{1,0:T(8,128)(2,1)}, f32[512,512]{1,0:T(8,128)}, f32[1,64]{1,0:T(1,128)}, f32[1,64]{1,0:T(1,128)}, f32[64,128]{1,0:T(8,128)}, /*index=...) custom-call(f32[64,384]{1,0:T(8,128)} %get-tuple-element.33.refs_0_,, ...), custom_call_target="tpu_custom_call" | custom-call | tf_op jit(solution)/shard_map/unpack/pallas_call | solution.py:1211

commit v3 on v2

--- a/solution.py
+++ b/solution.py
@@ -243,7 +243,7 @@
         chosen = iota((32, LANES), 0) % 8 == 2 * p + iota((32, LANES), 1) // HEAD_DIM
         r.rb[p] = tn(run3, jnp.where(chosen, 1.0, 0.0).astype(BF))
 
-    pair_loop(spread)
+    pair_loop(spread, PAIRS)
 
 
 def features(T, r, p, u, out):
@@ -453,7 +453,7 @@
 
 def up_grads(T, base, r):
     up, _ = feed_columns(r)
-    pair_loop(lambda p: put_panel(r.ggf, p, up, tn(r.two[...], r.gh[p])))
+    pair_loop(lambda p: put_panel(r.ggf, p, up, tn(r.two[...], r.gh[p])), PAIRS)
 
 
 def down_grads(T, base, r):
@@ -463,7 +463,7 @@
         put_panel(r.ggf, p, down, tn(r.cot[...], r.act[p]))
         put_panel(r.ggf, p, out_columns(r), tn(r.gb[...], r.att[p]))
 
-    pair_loop(part)
+    pair_loop(part, PAIRS)
 
 
 def put_panel(ref, p, cols, x):

time: 124 us -> 122 us (0.984)
    pallas_call x1, Pallas kernels: 119 us -> 118 us  [layer_near(): pl.pallas_call(functools.partial(layer_kernel, held, T * count, T), out_s...]
where the time goes in v3:
time: 122 us
  Pallas kernels  121 us (99%)
  between operations  1.37 us (1%)
    pallas_call x1, Pallas kernels, layer_near(): pl.pallas_call(functools.partial(layer_kernel, held, T * count, T), out_s...  118 us
    pallas_call x1, Pallas kernels, layer_near(): pl.pallas_call(unpacked, out_shape=shapes, in_specs=[vmem] * 5, out_specs...  2.85 us

profile of v3, /device:TPU:0, one launch (start us, length us, event | category | flops | bytes accessed | tf_op | source)
XLA Modules:
  0.0 122.1 jit_solution(15483783882789190453)
XLA Ops:
  1.3 117.9 %layer.1 = (bf16[512,512]{1,0:T(8,128)(2,1)}, f32[512,512]{1,0:T(8,128)}, f32[64,384]{1,0:T(8,128)}, f32[64,1152]{1,0:T(8,128)}, f32[8,128]{1,0:T(8,128)}) custom-call(s32[3]{0:T(128)} %lengths.1, s32[1]{0:T(128)S(6)} %copy.30.seed, f32[2]{0:T(128)} %bias.1, bf16[512,512]{1,0:T(8,128)(2,1)} %tok_in.1, bf16[512,512]{1,0:T(8,128)(2,1)} %cot_in.1, ...), custom_call_target="tpu_custom_call" | custom-call | tf_op jit(solution)/shard_map/layer/pallas_call | solution.py:1194
  119.2 2.8 %unpack.1 = (bf16[512,512]{1,0:T(8,128)(2,1)}, f32[512,512]{1,0:T(8,128)}, f32[1,64]{1,0:T(1,128)}, f32[1,64]{1,0:T(1,128)}, f32[64,128]{1,0:T(8,128)}, /*index=...) custom-call(f32[64,384]{1,0:T(8,128)} %get-tuple-element.33.refs_0_,, ...), custom_call_target="tpu_custom_call" | custom-call | tf_op jit(solution)/shard_map/unpack/pallas_call | solution.py:1211
